TPU v7x, 256 devices: a whole 4x4x8 slice. The times are simulated.
256 devices in a mesh: gx: 8 (over x, core), gyz: 8 (over y, z_lo), band: 4 (over z_hi).
Axes of the slice: x: 4, y: 4, z: 8 (z_hi: 4, z_lo: 2; z = z_hi * 2 + z_lo), core: 2. Of those that a mesh axis runs over, the one named last changes fastest.
Arguments:
- orbitals: float32 [256, 32, 64, 128], P('band', 'gx', 'gyz'), may hold values from -6 to 6
- v_local: float32 [32, 64, 128], P('gx', 'gyz'), may hold values from 0 to 2
- features: bfloat16 [11, 32, 64, 128], P(None, 'gx', 'gyz'), may hold values from -6 to 6
- w_first: bfloat16 [256, 11], replicated, may hold values from -1.75 to 1.75
- w_hidden: bfloat16 [1, 256, 256], replicated, may hold values from -0.375 to 0.375
- w_last: bfloat16 [256], replicated, may hold values from -0.375 to 0.375
- rotation: float32 [256, 256], replicated, may hold values from -0.375 to 0.375
- assignment: int32 [256], replicated, may hold values from 0 to 255, each once
- degrees: int32 [256], P('band'), may hold values from 4 to 8, as said below
Outputs:
- gram: float32 [256, 256], P('band')
- rotated: float32 [256, 32, 64, 128], P('band', 'gx', 'gyz')
Inputs may be any that keep to these rules, and one draw needn't show every extreme that they name: `degrees`: a filter degree of each slot; some slot has 8 and some has 4. `assignment`: each orbital is held in exactly one slot.
All inputs are finite; a program needn't handle non-finite values.
Results may differ from a plain program's by a relative error of at most 0.0043.
Values may be sent and summed in bfloat16 or wider, within the bound.
No kernel may reach another device: no remote copies, remote signals or barrier semaphores. Data moves between devices by JAX's collectives and lax.ppermute only.
A program may use at most 64 MiB of HBM per device.

v0:
```python
import jax
import jax.numpy as jnp
from jax import lax
from jax.sharding import PartitionSpec as P

DEG = 8
LOWER_EDGE = 2.0
CUT_EDGE = 3.0
UPPER_EDGE = 9.5


def with_halo(block, sides, width):
    for axis, dim in sides:
        count = lax.axis_size(axis)
        forward = [(i, i + 1) for i in range(count - 1)]
        backward = [(target, source) for source, target in forward]
        low = lax.ppermute(
            lax.slice_in_dim(block, block.shape[dim] - width, None, axis=dim), axis, forward
        )
        high = lax.ppermute(lax.slice_in_dim(block, 0, width, axis=dim), axis, backward)
        block = jnp.concatenate([low, block, high], axis=dim)
    return block


def coefficients(count):
    half_width = (UPPER_EDGE - CUT_EDGE) / 2.0
    centre = (UPPER_EDGE + CUT_EDGE) / 2.0
    first = half_width / (LOWER_EDGE - centre)
    factors = [(first / half_width, 0.0)]
    sigma = first
    for rounds in range(1, count):
        updated = 1.0 / (2.0 / first - sigma)
        factors.append((2.0 * updated / half_width, sigma * updated))
        sigma = updated
    return (factors, centre)


def hamiltonian(field, potential):
    padded = with_halo(field, (("gx", 1), ("gyz", 2)), 1)
    padded = jnp.pad(padded, ((0, 0), (0, 0), (0, 0), (1, 1)))
    beside_all = padded[:, 2:, 1:-1, 1:-1] + padded[:, :-2, 1:-1, 1:-1]
    beside_all = beside_all + padded[:, 1:-1, 2:, 1:-1] + padded[:, 1:-1, :-2, 1:-1]
    beside_all = beside_all + padded[:, 1:-1, 1:-1, 2:] + padded[:, 1:-1, 1:-1, :-2]
    return 0.5 * (6.0 * field - beside_all) + potential * field


def network(cell_features, w_first, w_hidden, w_last):
    feature_count = cell_features.shape[0]
    flattened = cell_features.reshape(feature_count, -1)
    hidden = jax.nn.silu(jnp.dot(w_first, flattened, preferred_element_type=jnp.float32)).astype(
        jnp.bfloat16
    )
    hidden = jax.nn.silu(jnp.dot(w_hidden[0], hidden, preferred_element_type=jnp.float32)).astype(
        jnp.bfloat16
    )
    values = jnp.tanh(jnp.dot(w_last[None, :], hidden, preferred_element_type=jnp.float32)[0])
    return values.reshape(cell_features.shape[1:])


def on_device(
    orbitals, v_local, features, w_first, w_hidden, w_last, rotation, assignment, degrees
):
    group = lax.axis_index("band")
    local_slots, size_x, size_y, size_z = orbitals.shape
    total_slots = rotation.shape[0]
    cells = size_x * size_y * size_z
    total_cells = float(cells * lax.axis_size("gx") * lax.axis_size("gyz"))
    xc_field = network(features, w_first, w_hidden, w_last)
    potential = v_local + xc_field
    factors, centre = coefficients(DEG)
    previous = orbitals
    current = orbitals
    for rounds in range(DEG):
        image = hamiltonian(current, potential)
        scale_new, scale_old = factors[rounds]
        updated = scale_new * (image - centre * current) - scale_old * previous
        active = (degrees > rounds)[:, None, None, None]
        previous = jnp.where(active, current, previous)
        current = jnp.where(active, updated, current)
    filtered = current.astype(jnp.bfloat16).reshape(local_slots, cells)
    select = (assignment[:, None] == lax.iota(jnp.int32, total_slots)[None, :]).astype(jnp.float32)
    permuted = jnp.dot(select, rotation, precision=lax.Precision.HIGHEST)
    slot_rotation = jnp.dot(permuted, select.T, precision=lax.Precision.HIGHEST).astype(
        jnp.bfloat16
    )
    own_columns = lax.dynamic_slice_in_dim(slot_rotation, group * local_slots, local_slots, 1)
    shard_rows = lax.all_gather(filtered, "band", axis=0, tiled=True)
    margin = lax.dot_general(
        filtered, shard_rows, (((1,), (1,)), ((), ())), preferred_element_type=jnp.float32
    )
    gram_part = margin
    rotated_part = lax.dot_general(
        own_columns, shard_rows, (((0,), (0,)), ((), ())), preferred_element_type=jnp.float32
    )
    gram_part, rotated_flat = (gram_part, rotated_part)
    gram = lax.psum(gram_part, ("gx", "gyz")) / total_cells
    rotated = rotated_flat.reshape(local_slots, size_x, size_y, size_z)
    return (gram, rotated)


def solution(mesh):
    placed = (
        P("band", "gx", "gyz", None),
        P("gx", "gyz", None),
        P(None, "gx", "gyz", None),
        P(),
        P(),
        P(),
        P(),
        P(),
        P("band"),
    )
    return jax.shard_map(
        on_device,
        mesh=mesh,
        in_specs=placed,
        out_specs=(P("band", None), P("band", "gx", "gyz", None)),
        check_vma=False,
    )
```

profile of v0, /device:TPU:8, one launch (start us, length us, event | category | flops | bytes accessed | tf_op | source)
XLA Modules:
  0.0 750.5 jit_solution(973591448265603997)
XLA Ops:
  7.2 1.9 copy.25
  9.1 1.8 collective-permute-start.1
  13.8 3.4 multiply_convert_fusion.1
  17.3 3.3 fusion.1
  21.3 3.7 collective-permute-start.2
  25.1 2.1 collective-permute-start.3
  27.2 2.1 collective-permute-done.2
  29.3 6.6 collective-permute-done.3
  39.2 3.0 collective-permute-start.5
  43.4 2.0 collective-permute-start.6
  45.5 3.8 collective-permute-start.7
  49.3 1.7 collective-permute-done.6
  51.0 3.5 collective-permute-done.7
  54.5 2.1 select_maximum_fusion.24
  59.2 4.8 collective-permute-start.9
  65.1 1.9 collective-permute-start.10
  67.1 3.9 collective-permute-start.11
  72.7 4.7 collective-permute-done.11
  77.4 2.1 select_maximum_fusion.20
  82.6 5.3 collective-permute-start.13
  89.0 1.9 collective-permute-start.14
  91.0 4.1 collective-permute-start.15
  96.6 4.7 collective-permute-done.15
  101.3 2.1 select_maximum_fusion.16
  103.5 1.8 fusion.49
  106.7 5.3 collective-permute-start.17
  113.1 1.9 collective-permute-start.18
  115.0 3.9 collective-permute-start.19
  120.7 4.7 collective-permute-done.19
  125.4 2.1 select_maximum_fusion.12
  130.1 5.3 collective-permute-start.21
  136.6 1.9 collective-permute-start.22
  138.5 3.9 collective-permute-start.23
  144.2 4.7 collective-permute-done.23
  148.9 2.1 select_maximum_fusion.8
  154.0 5.3 collective-permute-start.25
  160.4 1.9 collective-permute-start.26
  162.3 3.9 collective-permute-start.27
  168.0 4.7 collective-permute-done.27
  172.7 2.1 select_maximum_fusion.4
  177.4 5.3 collective-permute-start.29
  183.9 1.9 collective-permute-start.30
  185.8 3.9 collective-permute-start.31
  191.4 4.7 collective-permute-done.31
  196.2 2.1 select_maximum_fusion
  201.8 60.9 %all-gather.2.cloned.1.call-done = bf16[256,4096]{1,0:T(8,128)(2,1)} async-done(((bf16[64,4096]{1,0:T(8,128)(2,1)}), bf16[256,4096]{1,0:T(8,128)(2,1)}) %all-gather.2.cloned.1.call-update) | async-done | bytes 2097168 | tf_op jit(solution)/shard_map/all_gather | solution.py:87
  262.7 3.2 fusion.91
  267.6 474.6 %all-reduce.10.cloned.1.call-done = f32[64,256]{1,0:T(8,128)} async-done(((f32[64,256]{1,0:T(8,128)}), f32[64,256]{1,0:T(8,128)}) %all-reduce.10.cloned.1.call-update) | async-done | bytes 65552 | tf_op jit(solution)/shard_map/psum | solution.py:96
  (85 shorter events, 46.5 us)
Async XLA Ops:
  7.2 194.0 %copy-start = (f32[256,256]{1,0:T(8,128)S(1)}, f32[256,256]{1,0:T(8,128)}, u32[]{:S(2)}) copy-start(f32[256,256]{1,0:T(8,128)} %param.15) | copy-start | bytes 786436
  7.2 255.5 %all-gather.2.cloned.1.call-start = ((), (), s32[]{:S(2)}) async-start(), calls=%async_computation | async-start | bytes 2621440 | tf_op jit(solution)/shard_map/all_gather | solution.py:87
  9.1 11.5 %collective-permute-start.1 = (f32[64,1,8,128]{3,0,2,1:T(8,128)S(1)}, f32[64,1,8,128]{3,0,2,1:T(8,128)S(1)}, u32[]{:S(2)}, u32[]{:S(2)}) collective-permute-start(f32[64,1,8,128]{3,0,2,1:T(8,128)S(1)} %get-tuple-element.37), channel_id=1, source_target_pairs={{0,32},{32,64},{64,96},{96,128},{128,160},{160,192},{192,224},{1,3... | collective-permute-start | bytes 786440 | tf_op jit(solution)/shard_map/ppermute | solution.py:17
  10.9 10.4 %collective-permute-start = (f32[64,1,8,128]{3,0,2,1:T(8,128)S(1)}, f32[64,1,8,128]{3,0,2,1:T(8,128)S(1)}, u32[]{:S(2)}, u32[]{:S(2)}) collective-permute-start(f32[64,1,8,128]{3,0,2,1:T(8,128)S(1)} %get-tuple-element.36), channel_id=1, source_target_pairs={{32,0},{64,32},{96,64},{128,96},{160,128},{192,160},{224,192},{33,... | collective-permute-start | bytes 786440 | tf_op jit(solution)/shard_map/ppermute | solution.py:20
  17.3 3.3 copy-start.3
  17.3 3.4 copy-start.1
  20.6 6.6 copy-start.5
  21.3 8.0 %collective-permute-start.2 = (f32[64,6,1,128]{3,0,2,1:T(8,128)S(1)}, f32[64,6,1,128]{3,0,2,1:T(8,128)S(1)}, u32[]{:S(2)}, u32[]{:S(2)}) collective-permute-start(f32[64,6,1,128]{3,0,2,1:T(8,128)S(1)} %get-tuple-element.21), channel_id=1, source_target_pairs={{4,0},{8,4},{12,8},{16,12},{20,16},{24,20},{28,24},{5,1},{9,5},{13... | collective-permute-start | bytes 589832 | tf_op jit(solution)/shard_map/ppermute | solution.py:20
  25.1 10.9 %collective-permute-start.3 = (f32[64,6,1,128]{3,0,2,1:T(8,128)S(1)}, f32[64,6,1,128]{3,0,2,1:T(8,128)S(1)}, u32[]{:S(2)}, u32[]{:S(2)}) collective-permute-start(f32[64,6,1,128]{3,0,2,1:T(8,128)S(1)} %get-tuple-element.20), channel_id=1, source_target_pairs={{0,4},{4,8},{8,12},{12,16},{16,20},{20,24},{24,28},{1,5},{5,9},{9,... | collective-permute-start | bytes 589832 | tf_op jit(solution)/shard_map/ppermute | solution.py:17
  37.9 4.4 collective-permute-start.4
  39.2 4.2 collective-permute-start.5
  43.4 7.6 %collective-permute-start.6 = (f32[64,6,1,128]{3,0,2,1:T(8,128)S(1)}, f32[64,6,1,128]{3,0,2,1:T(8,128)S(1)}, u32[]{:S(2)}, u32[]{:S(2)}) collective-permute-start(f32[64,6,1,128]{3,0,2,1:T(8,128)S(1)} %get-tuple-element.19), channel_id=1, source_target_pairs={{4,0},{8,4},{12,8},{16,12},{20,16},{24,20},{28,24},{5,1},{9,5},{13... | collective-permute-start | bytes 589832 | tf_op jit(solution)/shard_map/ppermute | solution.py:20
  45.5 9.0 %collective-permute-start.7 = (f32[64,6,1,128]{3,0,2,1:T(8,128)S(1)}, f32[64,6,1,128]{3,0,2,1:T(8,128)S(1)}, u32[]{:S(2)}, u32[]{:S(2)}) collective-permute-start(f32[64,6,1,128]{3,0,2,1:T(8,128)S(1)} %get-tuple-element.18), channel_id=1, source_target_pairs={{0,4},{4,8},{8,12},{12,16},{16,20},{20,24},{24,28},{1,5},{5,9},{9,... | collective-permute-start | bytes 589832 | tf_op jit(solution)/shard_map/ppermute | solution.py:17
  57.9 6.1 collective-permute-start.8
  59.2 5.9 collective-permute-start.9
  65.1 7.6 %collective-permute-start.10 = (f32[64,6,1,128]{3,0,2,1:T(8,128)S(1)}, f32[64,6,1,128]{3,0,2,1:T(8,128)S(1)}, u32[]{:S(2)}, u32[]{:S(2)}) collective-permute-start(f32[64,6,1,128]{3,0,2,1:T(8,128)S(1)} %get-tuple-element.17), channel_id=1, source_target_pairs={{4,0},{8,4},{12,8},{16,12},{20,16},{24,20},{28,24},{5,1},{9,5},{13... | collective-permute-start | bytes 589832 | tf_op jit(solution)/shard_map/ppermute | solution.py:20
  67.1 10.4 %collective-permute-start.11 = (f32[64,6,1,128]{3,0,2,1:T(8,128)S(1)}, f32[64,6,1,128]{3,0,2,1:T(8,128)S(1)}, u32[]{:S(2)}, u32[]{:S(2)}) collective-permute-start(f32[64,6,1,128]{3,0,2,1:T(8,128)S(1)} %get-tuple-element.16), channel_id=1, source_target_pairs={{0,4},{4,8},{8,12},{12,16},{16,20},{20,24},{24,28},{1,5},{5,9},{9,... | collective-permute-start | bytes 589832 | tf_op jit(solution)/shard_map/ppermute | solution.py:17
  81.3 6.6 collective-permute-start.12
  82.6 6.4 collective-permute-start.13
  89.0 7.6 %collective-permute-start.14 = (f32[64,6,1,128]{3,0,2,1:T(8,128)S(1)}, f32[64,6,1,128]{3,0,2,1:T(8,128)S(1)}, u32[]{:S(2)}, u32[]{:S(2)}) collective-permute-start(f32[64,6,1,128]{3,0,2,1:T(8,128)S(1)} %get-tuple-element.15), channel_id=1, source_target_pairs={{4,0},{8,4},{12,8},{16,12},{20,16},{24,20},{28,24},{5,1},{9,5},{13... | collective-permute-start | bytes 589832 | tf_op jit(solution)/shard_map/ppermute | solution.py:20
  91.0 10.4 %collective-permute-start.15 = (f32[64,6,1,128]{3,0,2,1:T(8,128)S(1)}, f32[64,6,1,128]{3,0,2,1:T(8,128)S(1)}, u32[]{:S(2)}, u32[]{:S(2)}) collective-permute-start(f32[64,6,1,128]{3,0,2,1:T(8,128)S(1)} %get-tuple-element.14), channel_id=1, source_target_pairs={{0,4},{4,8},{8,12},{12,16},{16,20},{20,24},{24,28},{1,5},{5,9},{9,... | collective-permute-start | bytes 589832 | tf_op jit(solution)/shard_map/ppermute | solution.py:17
  105.4 6.6 collective-permute-start.16
  106.7 6.4 collective-permute-start.17
  113.1 7.6 %collective-permute-start.18 = (f32[64,6,1,128]{3,0,2,1:T(8,128)S(1)}, f32[64,6,1,128]{3,0,2,1:T(8,128)S(1)}, u32[]{:S(2)}, u32[]{:S(2)}) collective-permute-start(f32[64,6,1,128]{3,0,2,1:T(8,128)S(1)} %get-tuple-element.13), channel_id=1, source_target_pairs={{4,0},{8,4},{12,8},{16,12},{20,16},{24,20},{28,24},{5,1},{9,5},{13... | collective-permute-start | bytes 589832 | tf_op jit(solution)/shard_map/ppermute | solution.py:20
  115.0 10.4 %collective-permute-start.19 = (f32[64,6,1,128]{3,0,2,1:T(8,128)S(1)}, f32[64,6,1,128]{3,0,2,1:T(8,128)S(1)}, u32[]{:S(2)}, u32[]{:S(2)}) collective-permute-start(f32[64,6,1,128]{3,0,2,1:T(8,128)S(1)} %get-tuple-element.12), channel_id=1, source_target_pairs={{0,4},{4,8},{8,12},{12,16},{16,20},{20,24},{24,28},{1,5},{5,9},{9,... | collective-permute-start | bytes 589832 | tf_op jit(solution)/shard_map/ppermute | solution.py:17
  128.8 6.6 collective-permute-start.20
  130.1 6.4 collective-permute-start.21
  136.6 7.6 %collective-permute-start.22 = (f32[64,6,1,128]{3,0,2,1:T(8,128)S(1)}, f32[64,6,1,128]{3,0,2,1:T(8,128)S(1)}, u32[]{:S(2)}, u32[]{:S(2)}) collective-permute-start(f32[64,6,1,128]{3,0,2,1:T(8,128)S(1)} %get-tuple-element.11), channel_id=1, source_target_pairs={{4,0},{8,4},{12,8},{16,12},{20,16},{24,20},{28,24},{5,1},{9,5},{13... | collective-permute-start | bytes 589832 | tf_op jit(solution)/shard_map/ppermute | solution.py:20
  138.5 10.4 %collective-permute-start.23 = (f32[64,6,1,128]{3,0,2,1:T(8,128)S(1)}, f32[64,6,1,128]{3,0,2,1:T(8,128)S(1)}, u32[]{:S(2)}, u32[]{:S(2)}) collective-permute-start(f32[64,6,1,128]{3,0,2,1:T(8,128)S(1)} %get-tuple-element.10), channel_id=1, source_target_pairs={{0,4},{4,8},{8,12},{12,16},{16,20},{20,24},{24,28},{1,5},{5,9},{9,... | collective-permute-start | bytes 589832 | tf_op jit(solution)/shard_map/ppermute | solution.py:17
  152.7 6.6 collective-permute-start.24
  154.0 6.4 collective-permute-start.25
  160.4 7.6 %collective-permute-start.26 = (f32[64,6,1,128]{3,0,2,1:T(8,128)S(1)}, f32[64,6,1,128]{3,0,2,1:T(8,128)S(1)}, u32[]{:S(2)}, u32[]{:S(2)}) collective-permute-start(f32[64,6,1,128]{3,0,2,1:T(8,128)S(1)} %get-tuple-element.9), channel_id=1, source_target_pairs={{4,0},{8,4},{12,8},{16,12},{20,16},{24,20},{28,24},{5,1},{9,5},{13... | collective-permute-start | bytes 589832 | tf_op jit(solution)/shard_map/ppermute | solution.py:20
  162.3 10.4 %collective-permute-start.27 = (f32[64,6,1,128]{3,0,2,1:T(8,128)S(1)}, f32[64,6,1,128]{3,0,2,1:T(8,128)S(1)}, u32[]{:S(2)}, u32[]{:S(2)}) collective-permute-start(f32[64,6,1,128]{3,0,2,1:T(8,128)S(1)} %get-tuple-element.8), channel_id=1, source_target_pairs={{0,4},{4,8},{8,12},{12,16},{16,20},{20,24},{24,28},{1,5},{5,9},{9,... | collective-permute-start | bytes 589832 | tf_op jit(solution)/shard_map/ppermute | solution.py:17
  176.1 6.6 collective-permute-start.28
  177.4 6.4 collective-permute-start.29
  183.9 7.6 %collective-permute-start.30 = (f32[64,6,1,128]{3,0,2,1:T(8,128)S(1)}, f32[64,6,1,128]{3,0,2,1:T(8,128)S(1)}, u32[]{:S(2)}, u32[]{:S(2)}) collective-permute-start(f32[64,6,1,128]{3,0,2,1:T(8,128)S(1)} %get-tuple-element.7), channel_id=1, source_target_pairs={{4,0},{8,4},{12,8},{16,12},{20,16},{24,20},{28,24},{5,1},{9,5},{13... | collective-permute-start | bytes 589832 | tf_op jit(solution)/shard_map/ppermute | solution.py:20
  185.8 10.4 %collective-permute-start.31 = (f32[64,6,1,128]{3,0,2,1:T(8,128)S(1)}, f32[64,6,1,128]{3,0,2,1:T(8,128)S(1)}, u32[]{:S(2)}, u32[]{:S(2)}) collective-permute-start(f32[64,6,1,128]{3,0,2,1:T(8,128)S(1)} %get-tuple-element.6), channel_id=1, source_target_pairs={{0,4},{4,8},{8,12},{12,16},{16,20},{20,24},{24,28},{1,5},{5,9},{9,... | collective-permute-start | bytes 589832 | tf_op jit(solution)/shard_map/ppermute | solution.py:17
  198.3 2.8 copy-start.4
  201.1 541.1 %all-reduce.10.cloned.1.call-start = ((), (), s32[]{:S(2)}) async-start(), calls=%async_computation.1 | async-start | bytes 131072 | tf_op jit(solution)/shard_map/psum | solution.py:96
  262.7 3.2 copy-start.2
Sparse Core Ops, SparseCore 0:
  201.2 61.4 all-gather.1
  266.0 476.0 all-reduce.9
where the time goes:
time: 752 us; the launch traced here: 750 us
  waiting for transfers between devices  596 us (79%)
  starting transfers between devices  93.3 us (12%)
  other arithmetic  28.6 us (4%)
  between operations  14.7 us (2%)
  matrix products  11 us (1%)
    psum x1, waiting for transfers between devices, on_device(): gram = lax.psum(gram_part, ('gx', 'gyz')) / total_cells  475 us
    ppermute x16, starting transfers between devices, with_halo(): lax.ppermute(lax.slice_in_dim(block, block.shape[dim] - width, None, axis...  65.6 us
    all_gather x1, waiting for transfers between devices, on_device(): shard_rows = lax.all_gather(filtered, 'band', axis=0, tiled=True)  60.9 us
    ppermute x16, waiting for transfers between devices, with_halo(): lax.ppermute(lax.slice_in_dim(block, block.shape[dim] - width, None, axis...  46.3 us
    ppermute x16, starting transfers between devices, with_halo(): lax.ppermute(lax.slice_in_dim(block, 0, width, axis=dim), axis, backward)  27.6 us
    concatenate x15, other arithmetic, with_halo(): block = jnp.concatenate([low, block, high], axis=dim)  16.2 us
  transfers between devices with their start and end apart: 34, of which 25 were waited for; matrix products, arithmetic and copies ran while one was open for 2% of the time, Pallas kernels for 0%

commit v1 on v0

--- a/solution.py
+++ b/solution.py
@@ -93,7 +93,7 @@
         own_columns, shard_rows, (((0,), (0,)), ((), ())), preferred_element_type=jnp.float32
     )
     gram_part, rotated_flat = (gram_part, rotated_part)
-    gram = lax.psum(gram_part, ("gx", "gyz")) / total_cells
+    gram = lax.psum(lax.psum(gram_part, "gyz"), "gx") / total_cells
     rotated = rotated_flat.reshape(local_slots, size_x, size_y, size_z)
     return (gram, rotated)
 

time: 752 us -> 415 us (0.55)
  waiting for transfers between devices: 596 us -> 260 us
    psum x1 -> x2, waiting for transfers between devices: 475 us -> 138 us  [on_device(): gram = lax.psum(lax.psum(gram_part, 'gyz'), 'gx') / total_cells]
  transfers between devices with their start and end apart: 34 -> 35, of which waited for: 25 -> 26; matrix products, arithmetic and copies ran while one was open for 2% -> 3% of each run, Pallas kernels for 0% -> 0%
where the time goes in v1:
time: 415 us; the launch traced here: 414 us
  waiting for transfers between devices  260 us (63%)
  starting transfers between devices  93.4 us (23%)
  other arithmetic  28.6 us (7%)
  between operations  14.4 us (3%)
  matrix products  11 us (3%)
  local copies, waits for them, and re-layouts  7.04 us (2%)
    psum x2, waiting for transfers between devices, on_device(): gram = lax.psum(lax.psum(gram_part, 'gyz'), 'gx') / total_cells  138 us
    ppermute x16, starting transfers between devices, with_halo(): lax.ppermute(lax.slice_in_dim(block, block.shape[dim] - width, None, axis...  65.6 us
    all_gather x1, waiting for transfers between devices, on_device(): shard_rows = lax.all_gather(filtered, 'band', axis=0, tiled=True)  61.2 us
    ppermute x16, waiting for transfers between devices, with_halo(): lax.ppermute(lax.slice_in_dim(block, block.shape[dim] - width, None, axis...  46.3 us
    ppermute x16, starting transfers between devices, with_halo(): lax.ppermute(lax.slice_in_dim(block, 0, width, axis=dim), axis, backward)  27.6 us
    concatenate x15, other arithmetic, with_halo(): block = jnp.concatenate([low, block, high], axis=dim)  16.2 us
    ppermute x16, waiting for transfers between devices, with_halo(): lax.ppermute(lax.slice_in_dim(block, 0, width, axis=dim), axis, backward)  13.9 us
    select_n x7, other arithmetic, on_device(): current = jnp.where(active, updated, current)  9.57 us
  transfers between devices with their start and end apart: 35, of which 26 were waited for; matrix products, arithmetic and copies ran while one was open for 3% of the time, Pallas kernels for 0%

profile of v1, /device:TPU:8, one launch (start us, length us, event | category | flops | bytes accessed | tf_op | source)
XLA Modules:
  0.0 414.3 jit_solution(16508075929327226018)
XLA Ops:
  7.2 1.9 copy.25
  9.1 1.8 collective-permute-start.1
  13.8 3.4 multiply_convert_fusion.1
  17.3 3.3 fusion.1
  21.3 3.7 collective-permute-start.2
  25.1 2.1 collective-permute-start.3
  27.2 2.1 collective-permute-done.2
  29.3 6.6 %collective-permute-done.3 = f32[64,6,1,128]{3,0,2,1:T(8,128)S(1)} collective-permute-done((f32[64,6,1,128]{3,0,2,1:T(8,128)S(1)}, f32[64,6,1,128]{3,0,2,1:T(8,128)S(1)}, u32[]{:S(2)}, u32[]{:S(2)}) %collective-permute-start.3) | collective-permute-done | bytes 196640 | tf_op jit(solution)/shard_map/ppermute | solution.py:17
  39.2 3.0 collective-permute-start.5
  43.4 2.0 collective-permute-start.6
  45.5 3.8 collective-permute-start.7
  51.0 3.5 collective-permute-done.7
  54.5 2.1 select_maximum_fusion.24
  59.2 4.8 %collective-permute-start.9 = (f32[64,1,8,128]{3,0,2,1:T(8,128)S(1)}, f32[64,1,8,128]{3,0,2,1:T(8,128)S(1)}, u32[]{:S(2)}, u32[]{:S(2)}) collective-permute-start(f32[64,1,8,128]{3,0,2,1:T(8,128)S(1)} %get-tuple-element.32), channel_id=1, source_target_pairs={{0,32},{32,64},{64,96},{96,128},{128,160},{160,192},{192,224},{1,3... | collective-permute-start | bytes 786440 | tf_op jit(solution)/shard_map/ppermute | solution.py:17
  65.1 1.9 collective-permute-start.10
  67.1 3.9 collective-permute-start.11
  72.7 4.7 %collective-permute-done.11 = f32[64,6,1,128]{3,0,2,1:T(8,128)S(1)} collective-permute-done((f32[64,6,1,128]{3,0,2,1:T(8,128)S(1)}, f32[64,6,1,128]{3,0,2,1:T(8,128)S(1)}, u32[]{:S(2)}, u32[]{:S(2)}) %collective-permute-start.11) | collective-permute-done | bytes 196640 | tf_op jit(solution)/shard_map/ppermute | solution.py:17
  77.4 2.1 select_maximum_fusion.20
  82.6 5.3 %collective-permute-start.13 = (f32[64,1,8,128]{3,0,2,1:T(8,128)S(1)}, f32[64,1,8,128]{3,0,2,1:T(8,128)S(1)}, u32[]{:S(2)}, u32[]{:S(2)}) collective-permute-start(f32[64,1,8,128]{3,0,2,1:T(8,128)S(1)} %get-tuple-element.30), channel_id=1, source_target_pairs={{0,32},{32,64},{64,96},{96,128},{128,160},{160,192},{192,224},{1,3... | collective-permute-start | bytes 786440 | tf_op jit(solution)/shard_map/ppermute | solution.py:17
  89.0 1.9 collective-permute-start.14
  91.0 4.1 collective-permute-start.15
  96.6 4.7 %collective-permute-done.15 = f32[64,6,1,128]{3,0,2,1:T(8,128)S(1)} collective-permute-done((f32[64,6,1,128]{3,0,2,1:T(8,128)S(1)}, f32[64,6,1,128]{3,0,2,1:T(8,128)S(1)}, u32[]{:S(2)}, u32[]{:S(2)}) %collective-permute-start.15) | collective-permute-done | bytes 196640 | tf_op jit(solution)/shard_map/ppermute | solution.py:17
  101.3 2.1 select_maximum_fusion.16
  103.5 1.8 fusion.49
  106.7 5.3 %collective-permute-start.17 = (f32[64,1,8,128]{3,0,2,1:T(8,128)S(1)}, f32[64,1,8,128]{3,0,2,1:T(8,128)S(1)}, u32[]{:S(2)}, u32[]{:S(2)}) collective-permute-start(f32[64,1,8,128]{3,0,2,1:T(8,128)S(1)} %get-tuple-element.28), channel_id=1, source_target_pairs={{0,32},{32,64},{64,96},{96,128},{128,160},{160,192},{192,224},{1,3... | collective-permute-start | bytes 786440 | tf_op jit(solution)/shard_map/ppermute | solution.py:17
  113.1 1.9 collective-permute-start.18
  115.0 3.9 collective-permute-start.19
  120.7 4.7 %collective-permute-done.19 = f32[64,6,1,128]{3,0,2,1:T(8,128)S(1)} collective-permute-done((f32[64,6,1,128]{3,0,2,1:T(8,128)S(1)}, f32[64,6,1,128]{3,0,2,1:T(8,128)S(1)}, u32[]{:S(2)}, u32[]{:S(2)}) %collective-permute-start.19) | collective-permute-done | bytes 196640 | tf_op jit(solution)/shard_map/ppermute | solution.py:17
  125.4 2.1 select_maximum_fusion.12
  130.1 5.3 %collective-permute-start.21 = (f32[64,1,8,128]{3,0,2,1:T(8,128)S(1)}, f32[64,1,8,128]{3,0,2,1:T(8,128)S(1)}, u32[]{:S(2)}, u32[]{:S(2)}) collective-permute-start(f32[64,1,8,128]{3,0,2,1:T(8,128)S(1)} %get-tuple-element.26), channel_id=1, source_target_pairs={{0,32},{32,64},{64,96},{96,128},{128,160},{160,192},{192,224},{1,3... | collective-permute-start | bytes 786440 | tf_op jit(solution)/shard_map/ppermute | solution.py:17
  136.6 1.9 collective-permute-start.22
  138.5 3.9 collective-permute-start.23
  144.2 4.7 %collective-permute-done.23 = f32[64,6,1,128]{3,0,2,1:T(8,128)S(1)} collective-permute-done((f32[64,6,1,128]{3,0,2,1:T(8,128)S(1)}, f32[64,6,1,128]{3,0,2,1:T(8,128)S(1)}, u32[]{:S(2)}, u32[]{:S(2)}) %collective-permute-start.23) | collective-permute-done | bytes 196640 | tf_op jit(solution)/shard_map/ppermute | solution.py:17
  148.9 2.1 select_maximum_fusion.8
  154.0 5.3 %collective-permute-start.25 = (f32[64,1,8,128]{3,0,2,1:T(8,128)S(1)}, f32[64,1,8,128]{3,0,2,1:T(8,128)S(1)}, u32[]{:S(2)}, u32[]{:S(2)}) collective-permute-start(f32[64,1,8,128]{3,0,2,1:T(8,128)S(1)} %get-tuple-element.24), channel_id=1, source_target_pairs={{0,32},{32,64},{64,96},{96,128},{128,160},{160,192},{192,224},{1,3... | collective-permute-start | bytes 786440 | tf_op jit(solution)/shard_map/ppermute | solution.py:17
  160.4 1.9 collective-permute-start.26
  162.3 3.9 collective-permute-start.27
  168.0 4.7 %collective-permute-done.27 = f32[64,6,1,128]{3,0,2,1:T(8,128)S(1)} collective-permute-done((f32[64,6,1,128]{3,0,2,1:T(8,128)S(1)}, f32[64,6,1,128]{3,0,2,1:T(8,128)S(1)}, u32[]{:S(2)}, u32[]{:S(2)}) %collective-permute-start.27) | collective-permute-done | bytes 196640 | tf_op jit(solution)/shard_map/ppermute | solution.py:17
  172.7 2.1 select_maximum_fusion.4
  177.4 5.3 %collective-permute-start.29 = (f32[64,1,8,128]{3,0,2,1:T(8,128)S(1)}, f32[64,1,8,128]{3,0,2,1:T(8,128)S(1)}, u32[]{:S(2)}, u32[]{:S(2)}) collective-permute-start(f32[64,1,8,128]{3,0,2,1:T(8,128)S(1)} %get-tuple-element.22), channel_id=1, source_target_pairs={{0,32},{32,64},{64,96},{96,128},{128,160},{160,192},{192,224},{1,3... | collective-permute-start | bytes 786440 | tf_op jit(solution)/shard_map/ppermute | solution.py:17
  183.9 1.9 collective-permute-start.30
  185.8 3.9 collective-permute-start.31
  191.4 4.7 %collective-permute-done.31 = f32[64,6,1,128]{3,0,2,1:T(8,128)S(1)} collective-permute-done((f32[64,6,1,128]{3,0,2,1:T(8,128)S(1)}, f32[64,6,1,128]{3,0,2,1:T(8,128)S(1)}, u32[]{:S(2)}, u32[]{:S(2)}) %collective-permute-start.31) | collective-permute-done | bytes 196640 | tf_op jit(solution)/shard_map/ppermute | solution.py:17
  196.2 2.1 select_maximum_fusion
  201.5 61.2 %all-gather.2.cloned.1.call-done = bf16[256,4096]{1,0:T(8,128)(2,1)} async-done(((bf16[64,4096]{1,0:T(8,128)(2,1)}), bf16[256,4096]{1,0:T(8,128)(2,1)}) %all-gather.2.cloned.1.call-update) | async-done | bytes 2097168 | tf_op jit(solution)/shard_map/all_gather | solution.py:87
  262.7 3.1 fusion.91
  266.3 73.7 %all-reduce.11.cloned.1.call-done = f32[64,256]{1,0:T(8,128)} async-done(((f32[64,256]{1,0:T(8,128)}), f32[64,256]{1,0:T(8,128)}) %all-reduce.11.cloned.1.call-update) | async-done | bytes 65552 | tf_op jit(solution)/shard_map/psum | solution.py:96
  341.7 64.6 %all-reduce.13.cloned.1.call-done = f32[64,256]{1,0:T(8,128)} async-done(((f32[64,256]{1,0:T(8,128)}), f32[64,256]{1,0:T(8,128)}) %all-reduce.13.cloned.1.call-update) | async-done | bytes 65552 | tf_op jit(solution)/shard_map/psum | solution.py:96
  (88 shorter events, 48.3 us)
Async XLA Ops:
  7.2 194.0 %copy-start = (f32[256,256]{1,0:T(8,128)S(1)}, f32[256,256]{1,0:T(8,128)}, u32[]{:S(2)}) copy-start(f32[256,256]{1,0:T(8,128)} %param.15) | copy-start | bytes 786436
  7.2 255.5 %all-gather.2.cloned.1.call-start = ((), (), s32[]{:S(2)}) async-start(), calls=%async_computation | async-start | bytes 2621440 | tf_op jit(solution)/shard_map/all_gather | solution.py:87
  9.1 11.5 %collective-permute-start.1 = (f32[64,1,8,128]{3,0,2,1:T(8,128)S(1)}, f32[64,1,8,128]{3,0,2,1:T(8,128)S(1)}, u32[]{:S(2)}, u32[]{:S(2)}) collective-permute-start(f32[64,1,8,128]{3,0,2,1:T(8,128)S(1)} %get-tuple-element.37), channel_id=1, source_target_pairs={{0,32},{32,64},{64,96},{96,128},{128,160},{160,192},{192,224},{1,3... | collective-permute-start | bytes 786440 | tf_op jit(solution)/shard_map/ppermute | solution.py:17
  10.9 10.4 %collective-permute-start = (f32[64,1,8,128]{3,0,2,1:T(8,128)S(1)}, f32[64,1,8,128]{3,0,2,1:T(8,128)S(1)}, u32[]{:S(2)}, u32[]{:S(2)}) collective-permute-start(f32[64,1,8,128]{3,0,2,1:T(8,128)S(1)} %get-tuple-element.36), channel_id=1, source_target_pairs={{32,0},{64,32},{96,64},{128,96},{160,128},{192,160},{224,192},{33,... | collective-permute-start | bytes 786440 | tf_op jit(solution)/shard_map/ppermute | solution.py:20
  17.3 3.3 copy-start.3
  17.3 3.4 copy-start.1
  20.6 6.6 %copy-start.5 = (s32[64]{0:T(128)S(1)}, s32[64]{0:T(128)}, u32[]{:S(2)}) copy-start(s32[64]{0:T(128)} %param.17) | copy-start | bytes 772
  21.3 8.0 %collective-permute-start.2 = (f32[64,6,1,128]{3,0,2,1:T(8,128)S(1)}, f32[64,6,1,128]{3,0,2,1:T(8,128)S(1)}, u32[]{:S(2)}, u32[]{:S(2)}) collective-permute-start(f32[64,6,1,128]{3,0,2,1:T(8,128)S(1)} %get-tuple-element.21), channel_id=1, source_target_pairs={{4,0},{8,4},{12,8},{16,12},{20,16},{24,20},{28,24},{5,1},{9,5},{13... | collective-permute-start | bytes 589832 | tf_op jit(solution)/shard_map/ppermute | solution.py:20
  25.1 10.9 %collective-permute-start.3 = (f32[64,6,1,128]{3,0,2,1:T(8,128)S(1)}, f32[64,6,1,128]{3,0,2,1:T(8,128)S(1)}, u32[]{:S(2)}, u32[]{:S(2)}) collective-permute-start(f32[64,6,1,128]{3,0,2,1:T(8,128)S(1)} %get-tuple-element.20), channel_id=1, source_target_pairs={{0,4},{4,8},{8,12},{12,16},{16,20},{20,24},{24,28},{1,5},{5,9},{9,... | collective-permute-start | bytes 589832 | tf_op jit(solution)/shard_map/ppermute | solution.py:17
  37.9 4.4 %collective-permute-start.4 = (f32[64,1,8,128]{3,0,2,1:T(8,128)S(1)}, f32[64,1,8,128]{3,0,2,1:T(8,128)S(1)}, u32[]{:S(2)}, u32[]{:S(2)}) collective-permute-start(f32[64,1,8,128]{3,0,2,1:T(8,128)S(1)} %get-tuple-element.35), channel_id=1, source_target_pairs={{32,0},{64,32},{96,64},{128,96},{160,128},{192,160},{224,192},{33,... | collective-permute-start | bytes 786440 | tf_op jit(solution)/shard_map/ppermute | solution.py:20
  39.2 4.2 %collective-permute-start.5 = (f32[64,1,8,128]{3,0,2,1:T(8,128)S(1)}, f32[64,1,8,128]{3,0,2,1:T(8,128)S(1)}, u32[]{:S(2)}, u32[]{:S(2)}) collective-permute-start(f32[64,1,8,128]{3,0,2,1:T(8,128)S(1)} %get-tuple-element.34), channel_id=1, source_target_pairs={{0,32},{32,64},{64,96},{96,128},{128,160},{160,192},{192,224},{1,3... | collective-permute-start | bytes 786440 | tf_op jit(solution)/shard_map/ppermute | solution.py:17
  43.4 7.6 %collective-permute-start.6 = (f32[64,6,1,128]{3,0,2,1:T(8,128)S(1)}, f32[64,6,1,128]{3,0,2,1:T(8,128)S(1)}, u32[]{:S(2)}, u32[]{:S(2)}) collective-permute-start(f32[64,6,1,128]{3,0,2,1:T(8,128)S(1)} %get-tuple-element.19), channel_id=1, source_target_pairs={{4,0},{8,4},{12,8},{16,12},{20,16},{24,20},{28,24},{5,1},{9,5},{13... | collective-permute-start | bytes 589832 | tf_op jit(solution)/shard_map/ppermute | solution.py:20
  45.5 9.0 %collective-permute-start.7 = (f32[64,6,1,128]{3,0,2,1:T(8,128)S(1)}, f32[64,6,1,128]{3,0,2,1:T(8,128)S(1)}, u32[]{:S(2)}, u32[]{:S(2)}) collective-permute-start(f32[64,6,1,128]{3,0,2,1:T(8,128)S(1)} %get-tuple-element.18), channel_id=1, source_target_pairs={{0,4},{4,8},{8,12},{12,16},{16,20},{20,24},{24,28},{1,5},{5,9},{9,... | collective-permute-start | bytes 589832 | tf_op jit(solution)/shard_map/ppermute | solution.py:17
  57.9 6.1 %collective-permute-start.8 = (f32[64,1,8,128]{3,0,2,1:T(8,128)S(1)}, f32[64,1,8,128]{3,0,2,1:T(8,128)S(1)}, u32[]{:S(2)}, u32[]{:S(2)}) collective-permute-start(f32[64,1,8,128]{3,0,2,1:T(8,128)S(1)} %get-tuple-element.33), channel_id=1, source_target_pairs={{32,0},{64,32},{96,64},{128,96},{160,128},{192,160},{224,192},{33,... | collective-permute-start | bytes 786440 | tf_op jit(solution)/shard_map/ppermute | solution.py:20
  59.2 5.9 %collective-permute-start.9 = (f32[64,1,8,128]{3,0,2,1:T(8,128)S(1)}, f32[64,1,8,128]{3,0,2,1:T(8,128)S(1)}, u32[]{:S(2)}, u32[]{:S(2)}) collective-permute-start(f32[64,1,8,128]{3,0,2,1:T(8,128)S(1)} %get-tuple-element.32), channel_id=1, source_target_pairs={{0,32},{32,64},{64,96},{96,128},{128,160},{160,192},{192,224},{1,3... | collective-permute-start | bytes 786440 | tf_op jit(solution)/shard_map/ppermute | solution.py:17
  65.1 7.6 %collective-permute-start.10 = (f32[64,6,1,128]{3,0,2,1:T(8,128)S(1)}, f32[64,6,1,128]{3,0,2,1:T(8,128)S(1)}, u32[]{:S(2)}, u32[]{:S(2)}) collective-permute-start(f32[64,6,1,128]{3,0,2,1:T(8,128)S(1)} %get-tuple-element.17), channel_id=1, source_target_pairs={{4,0},{8,4},{12,8},{16,12},{20,16},{24,20},{28,24},{5,1},{9,5},{13... | collective-permute-start | bytes 589832 | tf_op jit(solution)/shard_map/ppermute | solution.py:20
  67.1 10.4 %collective-permute-start.11 = (f32[64,6,1,128]{3,0,2,1:T(8,128)S(1)}, f32[64,6,1,128]{3,0,2,1:T(8,128)S(1)}, u32[]{:S(2)}, u32[]{:S(2)}) collective-permute-start(f32[64,6,1,128]{3,0,2,1:T(8,128)S(1)} %get-tuple-element.16), channel_id=1, source_target_pairs={{0,4},{4,8},{8,12},{12,16},{16,20},{20,24},{24,28},{1,5},{5,9},{9,... | collective-permute-start | bytes 589832 | tf_op jit(solution)/shard_map/ppermute | solution.py:17
  81.3 6.6 %collective-permute-start.12 = (f32[64,1,8,128]{3,0,2,1:T(8,128)S(1)}, f32[64,1,8,128]{3,0,2,1:T(8,128)S(1)}, u32[]{:S(2)}, u32[]{:S(2)}) collective-permute-start(f32[64,1,8,128]{3,0,2,1:T(8,128)S(1)} %get-tuple-element.31), channel_id=1, source_target_pairs={{32,0},{64,32},{96,64},{128,96},{160,128},{192,160},{224,192},{33,... | collective-permute-start | bytes 786440 | tf_op jit(solution)/shard_map/ppermute | solution.py:20
  82.6 6.4 %collective-permute-start.13 = (f32[64,1,8,128]{3,0,2,1:T(8,128)S(1)}, f32[64,1,8,128]{3,0,2,1:T(8,128)S(1)}, u32[]{:S(2)}, u32[]{:S(2)}) collective-permute-start(f32[64,1,8,128]{3,0,2,1:T(8,128)S(1)} %get-tuple-element.30), channel_id=1, source_target_pairs={{0,32},{32,64},{64,96},{96,128},{128,160},{160,192},{192,224},{1,3... | collective-permute-start | bytes 786440 | tf_op jit(solution)/shard_map/ppermute | solution.py:17
  89.0 7.6 %collective-permute-start.14 = (f32[64,6,1,128]{3,0,2,1:T(8,128)S(1)}, f32[64,6,1,128]{3,0,2,1:T(8,128)S(1)}, u32[]{:S(2)}, u32[]{:S(2)}) collective-permute-start(f32[64,6,1,128]{3,0,2,1:T(8,128)S(1)} %get-tuple-element.15), channel_id=1, source_target_pairs={{4,0},{8,4},{12,8},{16,12},{20,16},{24,20},{28,24},{5,1},{9,5},{13... | collective-permute-start | bytes 589832 | tf_op jit(solution)/shard_map/ppermute | solution.py:20
  91.0 10.4 %collective-permute-start.15 = (f32[64,6,1,128]{3,0,2,1:T(8,128)S(1)}, f32[64,6,1,128]{3,0,2,1:T(8,128)S(1)}, u32[]{:S(2)}, u32[]{:S(2)}) collective-permute-start(f32[64,6,1,128]{3,0,2,1:T(8,128)S(1)} %get-tuple-element.14), channel_id=1, source_target_pairs={{0,4},{4,8},{8,12},{12,16},{16,20},{20,24},{24,28},{1,5},{5,9},{9,... | collective-permute-start | bytes 589832 | tf_op jit(solution)/shard_map/ppermute | solution.py:17
  105.4 6.6 %collective-permute-start.16 = (f32[64,1,8,128]{3,0,2,1:T(8,128)S(1)}, f32[64,1,8,128]{3,0,2,1:T(8,128)S(1)}, u32[]{:S(2)}, u32[]{:S(2)}) collective-permute-start(f32[64,1,8,128]{3,0,2,1:T(8,128)S(1)} %get-tuple-element.29), channel_id=1, source_target_pairs={{32,0},{64,32},{96,64},{128,96},{160,128},{192,160},{224,192},{33,... | collective-permute-start | bytes 786440 | tf_op jit(solution)/shard_map/ppermute | solution.py:20
  106.7 6.4 %collective-permute-start.17 = (f32[64,1,8,128]{3,0,2,1:T(8,128)S(1)}, f32[64,1,8,128]{3,0,2,1:T(8,128)S(1)}, u32[]{:S(2)}, u32[]{:S(2)}) collective-permute-start(f32[64,1,8,128]{3,0,2,1:T(8,128)S(1)} %get-tuple-element.28), channel_id=1, source_target_pairs={{0,32},{32,64},{64,96},{96,128},{128,160},{160,192},{192,224},{1,3... | collective-permute-start | bytes 786440 | tf_op jit(solution)/shard_map/ppermute | solution.py:17
  113.1 7.6 %collective-permute-start.18 = (f32[64,6,1,128]{3,0,2,1:T(8,128)S(1)}, f32[64,6,1,128]{3,0,2,1:T(8,128)S(1)}, u32[]{:S(2)}, u32[]{:S(2)}) collective-permute-start(f32[64,6,1,128]{3,0,2,1:T(8,128)S(1)} %get-tuple-element.13), channel_id=1, source_target_pairs={{4,0},{8,4},{12,8},{16,12},{20,16},{24,20},{28,24},{5,1},{9,5},{13... | collective-permute-start | bytes 589832 | tf_op jit(solution)/shard_map/ppermute | solution.py:20
  115.0 10.4 %collective-permute-start.19 = (f32[64,6,1,128]{3,0,2,1:T(8,128)S(1)}, f32[64,6,1,128]{3,0,2,1:T(8,128)S(1)}, u32[]{:S(2)}, u32[]{:S(2)}) collective-permute-start(f32[64,6,1,128]{3,0,2,1:T(8,128)S(1)} %get-tuple-element.12), channel_id=1, source_target_pairs={{0,4},{4,8},{8,12},{12,16},{16,20},{20,24},{24,28},{1,5},{5,9},{9,... | collective-permute-start | bytes 589832 | tf_op jit(solution)/shard_map/ppermute | solution.py:17
  128.8 6.6 %collective-permute-start.20 = (f32[64,1,8,128]{3,0,2,1:T(8,128)S(1)}, f32[64,1,8,128]{3,0,2,1:T(8,128)S(1)}, u32[]{:S(2)}, u32[]{:S(2)}) collective-permute-start(f32[64,1,8,128]{3,0,2,1:T(8,128)S(1)} %get-tuple-element.27), channel_id=1, source_target_pairs={{32,0},{64,32},{96,64},{128,96},{160,128},{192,160},{224,192},{33,... | collective-permute-start | bytes 786440 | tf_op jit(solution)/shard_map/ppermute | solution.py:20
  130.1 6.4 %collective-permute-start.21 = (f32[64,1,8,128]{3,0,2,1:T(8,128)S(1)}, f32[64,1,8,128]{3,0,2,1:T(8,128)S(1)}, u32[]{:S(2)}, u32[]{:S(2)}) collective-permute-start(f32[64,1,8,128]{3,0,2,1:T(8,128)S(1)} %get-tuple-element.26), channel_id=1, source_target_pairs={{0,32},{32,64},{64,96},{96,128},{128,160},{160,192},{192,224},{1,3... | collective-permute-start | bytes 786440 | tf_op jit(solution)/shard_map/ppermute | solution.py:17
  136.6 7.6 %collective-permute-start.22 = (f32[64,6,1,128]{3,0,2,1:T(8,128)S(1)}, f32[64,6,1,128]{3,0,2,1:T(8,128)S(1)}, u32[]{:S(2)}, u32[]{:S(2)}) collective-permute-start(f32[64,6,1,128]{3,0,2,1:T(8,128)S(1)} %get-tuple-element.11), channel_id=1, source_target_pairs={{4,0},{8,4},{12,8},{16,12},{20,16},{24,20},{28,24},{5,1},{9,5},{13... | collective-permute-start | bytes 589832 | tf_op jit(solution)/shard_map/ppermute | solution.py:20
  138.5 10.4 %collective-permute-start.23 = (f32[64,6,1,128]{3,0,2,1:T(8,128)S(1)}, f32[64,6,1,128]{3,0,2,1:T(8,128)S(1)}, u32[]{:S(2)}, u32[]{:S(2)}) collective-permute-start(f32[64,6,1,128]{3,0,2,1:T(8,128)S(1)} %get-tuple-element.10), channel_id=1, source_target_pairs={{0,4},{4,8},{8,12},{12,16},{16,20},{20,24},{24,28},{1,5},{5,9},{9,... | collective-permute-start | bytes 589832 | tf_op jit(solution)/shard_map/ppermute | solution.py:17
  152.7 6.6 %collective-permute-start.24 = (f32[64,1,8,128]{3,0,2,1:T(8,128)S(1)}, f32[64,1,8,128]{3,0,2,1:T(8,128)S(1)}, u32[]{:S(2)}, u32[]{:S(2)}) collective-permute-start(f32[64,1,8,128]{3,0,2,1:T(8,128)S(1)} %get-tuple-element.25), channel_id=1, source_target_pairs={{32,0},{64,32},{96,64},{128,96},{160,128},{192,160},{224,192},{33,... | collective-permute-start | bytes 786440 | tf_op jit(solution)/shard_map/ppermute | solution.py:20
  154.0 6.4 %collective-permute-start.25 = (f32[64,1,8,128]{3,0,2,1:T(8,128)S(1)}, f32[64,1,8,128]{3,0,2,1:T(8,128)S(1)}, u32[]{:S(2)}, u32[]{:S(2)}) collective-permute-start(f32[64,1,8,128]{3,0,2,1:T(8,128)S(1)} %get-tuple-element.24), channel_id=1, source_target_pairs={{0,32},{32,64},{64,96},{96,128},{128,160},{160,192},{192,224},{1,3... | collective-permute-start | bytes 786440 | tf_op jit(solution)/shard_map/ppermute | solution.py:17
  160.4 7.6 %collective-permute-start.26 = (f32[64,6,1,128]{3,0,2,1:T(8,128)S(1)}, f32[64,6,1,128]{3,0,2,1:T(8,128)S(1)}, u32[]{:S(2)}, u32[]{:S(2)}) collective-permute-start(f32[64,6,1,128]{3,0,2,1:T(8,128)S(1)} %get-tuple-element.9), channel_id=1, source_target_pairs={{4,0},{8,4},{12,8},{16,12},{20,16},{24,20},{28,24},{5,1},{9,5},{13... | collective-permute-start | bytes 589832 | tf_op jit(solution)/shard_map/ppermute | solution.py:20
  162.3 10.4 %collective-permute-start.27 = (f32[64,6,1,128]{3,0,2,1:T(8,128)S(1)}, f32[64,6,1,128]{3,0,2,1:T(8,128)S(1)}, u32[]{:S(2)}, u32[]{:S(2)}) collective-permute-start(f32[64,6,1,128]{3,0,2,1:T(8,128)S(1)} %get-tuple-element.8), channel_id=1, source_target_pairs={{0,4},{4,8},{8,12},{12,16},{16,20},{20,24},{24,28},{1,5},{5,9},{9,... | collective-permute-start | bytes 589832 | tf_op jit(solution)/shard_map/ppermute | solution.py:17
  176.1 6.6 %collective-permute-start.28 = (f32[64,1,8,128]{3,0,2,1:T(8,128)S(1)}, f32[64,1,8,128]{3,0,2,1:T(8,128)S(1)}, u32[]{:S(2)}, u32[]{:S(2)}) collective-permute-start(f32[64,1,8,128]{3,0,2,1:T(8,128)S(1)} %get-tuple-element.23), channel_id=1, source_target_pairs={{32,0},{64,32},{96,64},{128,96},{160,128},{192,160},{224,192},{33,... | collective-permute-start | bytes 786440 | tf_op jit(solution)/shard_map/ppermute | solution.py:20
  177.4 6.4 %collective-permute-start.29 = (f32[64,1,8,128]{3,0,2,1:T(8,128)S(1)}, f32[64,1,8,128]{3,0,2,1:T(8,128)S(1)}, u32[]{:S(2)}, u32[]{:S(2)}) collective-permute-start(f32[64,1,8,128]{3,0,2,1:T(8,128)S(1)} %get-tuple-element.22), channel_id=1, source_target_pairs={{0,32},{32,64},{64,96},{96,128},{128,160},{160,192},{192,224},{1,3... | collective-permute-start | bytes 786440 | tf_op jit(solution)/shard_map/ppermute | solution.py:17
  183.9 7.6 %collective-permute-start.30 = (f32[64,6,1,128]{3,0,2,1:T(8,128)S(1)}, f32[64,6,1,128]{3,0,2,1:T(8,128)S(1)}, u32[]{:S(2)}, u32[]{:S(2)}) collective-permute-start(f32[64,6,1,128]{3,0,2,1:T(8,128)S(1)} %get-tuple-element.7), channel_id=1, source_target_pairs={{4,0},{8,4},{12,8},{16,12},{20,16},{24,20},{28,24},{5,1},{9,5},{13... | collective-permute-start | bytes 589832 | tf_op jit(solution)/shard_map/ppermute | solution.py:20
  185.8 10.4 %collective-permute-start.31 = (f32[64,6,1,128]{3,0,2,1:T(8,128)S(1)}, f32[64,6,1,128]{3,0,2,1:T(8,128)S(1)}, u32[]{:S(2)}, u32[]{:S(2)}) collective-permute-start(f32[64,6,1,128]{3,0,2,1:T(8,128)S(1)} %get-tuple-element.6), channel_id=1, source_target_pairs={{0,4},{4,8},{8,12},{12,16},{16,20},{20,24},{24,28},{1,5},{5,9},{9,... | collective-permute-start | bytes 589832 | tf_op jit(solution)/shard_map/ppermute | solution.py:17
  198.3 2.8 copy-start.4
  201.1 138.9 %all-reduce.11.cloned.1.call-start = ((), (), s32[]{:S(2)}) async-start(), calls=%async_computation.1 | async-start | bytes 131072 | tf_op jit(solution)/shard_map/psum | solution.py:96
  262.7 77.3 %copy-start.2 = (bf16[256,4096]{1,0:T(8,128)(2,1)S(1)}, bf16[256,4096]{1,0:T(8,128)(2,1)}, u32[]{:S(2)}) copy-start(bf16[256,4096]{1,0:T(8,128)(2,1)} %all-gather.2.cloned.1.call-done) | copy-start | bytes 6291460
  265.9 140.4 %all-reduce.13.cloned.1.call-start = ((), (), s32[]{:S(2)}) async-start(), calls=%async_computation.2 | async-start | bytes 131072 | tf_op jit(solution)/shard_map/psum | solution.py:96
Sparse Core Ops, SparseCore 0:
  201.2 61.4 all-gather.1
  266.0 73.9 all-reduce.10
  342.4 63.7 all-reduce.12
